TPU v7x, 32 devices: a whole 2x2x4 slice. The times are simulated.
32 devices in a mesh: grp: 2 (over x), blk: 16 (over z, y, core).
Axes of the slice: x: 2, y: 2, z: 4, core: 2. Of those that a mesh axis runs over, the one named last changes fastest.
Arguments:
- doc_grads: float32 [24576, 2048], P(('grp', 'blk')), parts along dimension 0, may hold values from -250 to 250
- test_grads: float32 [512, 2048], P(('grp', 'blk')), parts along dimension 0, may hold values from -6 to 6
- eigen_basis: bfloat16 [2, 1024, 1024], replicated, may hold values from -0.1875 to 0.1875
- eigen_values: float32 [2, 1024], replicated, may hold values from 0.01 to 10
Outputs:
- influence: float32 [256, 24576], P(None, ('grp', 'blk')), parts along dimension 1
There are 2 independent parts, one for each index of `grp`. A program takes and returns all parts, laid end to end along the dimension named above; an argument that names none is the same for every part. Nothing has to cross between parts.
All inputs are finite; a program needn't handle non-finite values.
Results may differ from a plain program's by a relative error of at most 0.0029.
Values may be sent and summed in bfloat16 or wider, within the bound.
A program may use at most 128 MiB of HBM per device.

v0:
```python
import jax
import jax.numpy as jnp
from jax import lax
from jax.sharding import PartitionSpec as P


def precondition(rows, eigen_basis, eigen_values):
    layers = eigen_basis.shape[0]
    width = eigen_basis.shape[1]
    blocks = []
    for layer in range(layers):
        part = rows[:, layer * width : (layer + 1) * width]
        basis = eigen_basis[layer].astype(jnp.float32)
        values = eigen_values[layer]
        damping = 0.1 * jnp.mean(values)
        rotated = jnp.dot(
            part, basis, precision=lax.Precision.HIGHEST, preferred_element_type=jnp.float32
        )
        rotated = rotated / (values + damping)
        blocks.append(
            lax.dot_general(
                rotated,
                basis,
                (((1,), (1,)), ((), ())),
                precision=lax.Precision.HIGHEST,
                preferred_element_type=jnp.float32,
            )
        )
    return jnp.concatenate(blocks, axis=1).astype(jnp.bfloat16)


def score_rows(ready, doc_grads):
    return lax.dot_general(
        ready.astype(jnp.float32),
        doc_grads,
        (((1,), (1,)), ((), ())),
        precision=lax.Precision.HIGHEST,
        preferred_element_type=jnp.float32,
    )


def shards(doc_grads, test_grads, eigen_basis, eigen_values):
    raw = score_rows(
        precondition(
            lax.all_gather(test_grads, "blk", axis=0, tiled=True), eigen_basis, eigen_values
        ),
        doc_grads,
    )
    total_docs = doc_grads.shape[0] * lax.axis_size("blk")
    local_squares = jnp.sum(raw * raw, axis=1, keepdims=True)
    squares = lax.psum(local_squares, "blk")
    spread = squares / total_docs
    return raw / jnp.sqrt(spread + 1e-06)


def solution(mesh):
    in_specs = (P(("grp", "blk"), None), P(("grp", "blk"), None), P(), P())
    out_specs = P(None, ("grp", "blk"))
    return jax.shard_map(shards, mesh=mesh, in_specs=in_specs, out_specs=out_specs, check_vma=False)
```

profile of v0, /device:TPU:0, one launch (start us, length us, event | category | flops | bytes accessed | tf_op | source)
XLA Modules:
  0.0 105.9 jit_solution(6794357613871021474)
XLA Ops:
  6.5 0.0 all-gather.2.cloned.1.call-start
  6.5 0.7 all-gather.2.cloned.1.call-update
  7.3 1.4 %slice_reduce_fusion.1 = (f32[]{:T(128)}, f32[]{:T(128)}) fusion(f32[2,1024]{1,0:T(2,128)} %param.7), kind=kLoop, calls=%fused_computation.27 | loop fusion | flops 2046 | bytes 8200 | tf_op jit(solution)/shard_map/reduce_sum | solution.py:15
  9.9 0.8 slice_add_fusion.1
  10.7 42.9 %all-gather.2.cloned.1.call-done = f32[256,2048]{1,0:T(8,128)} async-done(((f32[16,2048]{1,0:T(8,128)}), f32[256,2048]{1,0:T(8,128)}) %all-gather.2.cloned.1.call-update) | async-done | bytes 2097168 | tf_op jit(solution)/shard_map/all_gather | solution.py:45
  53.7 0.0 copy-start
  53.7 0.0 copy-start.1
  53.7 3.9 %fusion.18 = f32[256,1024]{1,0:T(8,128)S(1)} fusion(bf16[2,1024,1024]{2,1,0:T(8,128)(2,1)} %param.6, f32[256,2048]{1,0:T(8,128)} %all-gather.2.cloned.1.call-done, f32[1024]{0:T(1024)S(1)} %bitcast.29), kind=kOutput, calls=%fused_computation.14 | convolution fusion | flops 3221487616 | bytes 4198400 | tf_op jit(solution)/shard_map/dot_general | solution.py:16
  57.5 0.0 copy-done
  57.5 0.0 slice-start
  57.6 1.9 %fusion.12 = bf16[256,1024]{1,0:T(8,128)(2,1)S(1)} fusion(f32[256,1024]{1,0:T(8,128)S(1)} %fusion.18, bf16[2,1024,1024]{2,1,0:T(8,128)(2,1)S(1)} %copy-done), kind=kOutput, calls=%fused_computation.12 | convolution fusion | flops 3221487616 | bytes 3670016 | tf_op jit(solution)/shard_map/dot_general | solution.py:21
  59.4 0.0 copy-done.1
  59.4 0.0 slice-start.1
  59.5 1.8 %fusion.21 = f32[256,1024]{1,0:T(8,128)S(1)} fusion(bf16[2,1024,1024]{2,1,0:T(8,128)(2,1)S(1)} %copy-done, f32[256,2048]{1,0:T(8,128)S(1)} %copy-done.1, f32[1024]{0:T(1024)S(1)} %bitcast.28), kind=kOutput, calls=%fused_computation.15 | convolution fusion | flops 3221487616 | bytes 4198400 | tf_op jit(solution)/shard_map/dot_general | solution.py:16
  61.3 1.9 %fusion.15 = bf16[256,1024]{1,0:T(8,128)(2,1)S(1)} fusion(f32[256,1024]{1,0:T(8,128)S(1)} %fusion.21, bf16[2,1024,1024]{2,1,0:T(8,128)(2,1)S(1)} %copy-done), kind=kOutput, calls=%fused_computation.13 | convolution fusion | flops 3221487616 | bytes 3670016 | tf_op jit(solution)/shard_map/dot_general | solution.py:21
  63.2 0.0 slice-done
  63.2 0.0 slice-done.1
  63.2 3.4 %multiply_reduce_fusion = (f32[256]{0:T(256)S(1)}, f32[256,768]{1,0:T(8,128)S(1)}) fusion(f32[768,2048]{1,0:T(8,128)S(1)} %bitcast.26, bf16[256,1024]{1,0:T(8,128)(2,1)S(1)} %fusion.15, bf16[256,1024]{1,0:T(8,128)(2,1)S(1)} %fusion.12), kind=kOutput, calls=%fused_computation.22 | convolution fusion | flops 4834328576 | bytes 8127488 | tf_op jit(solution)/shard_map/dot_general | solution.py:33
  66.6 31.4 %psum.7 = f32[256,1]{0,1:T(1,128)S(1)} all-reduce(f32[256,1]{0,1:T(1,128)S(1)} %bitcast.27), channel_id=1, replica_groups=mesh['grp'=2,'blk'=16] {'blk'}, use_global_device_ids=true, to_apply=%region_3.0 | all-reduce | flops 256 | bytes 2048 | tf_op jit(solution)/shard_map/psum | solution.py:51
  98.0 1.0 broadcast_divide_fusion
  (2 shorter events, 0.0 us)
Async XLA Ops:
  6.5 47.1 %all-gather.2.cloned.1.call-start = ((), (), s32[]{:S(2)}) async-start(), calls=%async_computation | async-start | bytes 2228224 | tf_op jit(solution)/shard_map/all_gather | solution.py:45
  53.7 3.9 %copy-start = (bf16[2,1024,1024]{2,1,0:T(8,128)(2,1)S(1)}, bf16[2,1024,1024]{2,1,0:T(8,128)(2,1)}, u32[]{:S(2)}) copy-start(bf16[2,1024,1024]{2,1,0:T(8,128)(2,1)} %param.6) | copy-start | bytes 12582916
  53.7 5.8 %copy-start.1 = (f32[256,2048]{1,0:T(8,128)S(1)}, f32[256,2048]{1,0:T(8,128)}, u32[]{:S(2)}) copy-start(f32[256,2048]{1,0:T(8,128)} %all-gather.2.cloned.1.call-done) | copy-start | bytes 6291460
  57.5 5.6 %slice-start = ((s8[6291456]{0:T(1024)(128)(4,1)}), s8[4194304]{0:T(1024)(128)(4,1)S(1)}, s32[]{:S(2)}) async-start(s8[6291456]{0:T(1024)(128)(4,1)} %bitcast.25), calls=%async_computation.1 | async-start | bytes 8388608
  59.4 3.7 %slice-start.1 = ((s8[6291456]{0:T(1024)(128)(4,1)}), s8[2097152]{0:T(1024)(128)(4,1)S(1)}, s32[]{:S(2)}) async-start(s8[6291456]{0:T(1024)(128)(4,1)} %bitcast.25), calls=%async_computation.2 | async-start | bytes 4194304
Sparse Core Ops, SparseCore 0:
  9.5 44.0 all-gather.1
where the time goes:
time: 106 us
  waiting for transfers between devices  43.6 us (41%)
  blocking collectives  31.4 us (30%)
  between operations  14.7 us (14%)
  matrix products  12.8 us (12%)
  other arithmetic  3.23 us (3%)
    all_gather x1, waiting for transfers between devices, shards(): lax.all_gather(test_grads, 'blk', axis=0, tiled=True)  42.9 us
    psum x1, blocking collectives, shards(): squares = lax.psum(local_squares, 'blk')  31.4 us
    dot_general x2, matrix products, precondition(): jnp.dot(part, basis, precision=lax.Precision.HIGHEST, preferred_element_t...  5.69 us
    dot_general x2, matrix products, precondition(): lax.dot_general(rotated, basis, (((1,), (1,)), ((), ())), precision=lax.P...  3.74 us
    dot_general x1, matrix products, score_rows(): lax.dot_general(ready.astype(jnp.float32), doc_grads, (((1,), (1,)), ((),...  3.37 us
  transfers between devices with their start and end apart: 1, of which 1 were waited for; matrix products, arithmetic and copies ran while one was open for 2% of the time, Pallas kernels for 0%

commit v1 on v0

v1 whole, which is shorter than its diff:
```python
import functools

import jax
import jax.numpy as jnp
from jax import lax
from jax.experimental import pallas as pl
from jax.experimental.pallas import tpu as pltpu
from jax.sharding import PartitionSpec as P

PIECES = 2
TILE = 256
MESH = pl.DeviceIdType.MESH
NT = (((1,), (1,)), ((), ()))


def repeat(count, body):
    if count <= 4:
        for i in range(count):
            body(i)
    else:
        lax.fori_loop(0, count, lambda i, c: (body(i), c)[1], 0)


def split3(x):
    high = x.astype(jnp.bfloat16)
    rest = x - high.astype(jnp.float32)
    mid = rest.astype(jnp.bfloat16)
    low = (rest - mid.astype(jnp.float32)).astype(jnp.bfloat16)
    return jnp.concatenate([high, mid, low], axis=0)


def kernel(
    far, near, docs_hbm, tests_hbm, basis_hbm, values_hbm, out_hbm,
    docs, tests, basis, values, ready, acc, sums,
    docs_sem, tests_sem, basis_sem, values_sem, out_sem,
    send_sem, recv_sem, sums_send, sums_recv,
):
    n = far * near * 2
    layers, width = values.shape
    chunks, _, rows, part = ready.shape
    total_docs = n * docs.shape[1]
    queries = n * rows
    me = lax.axis_index("blk")
    c = lax.rem(me, 2)
    b = lax.rem(me // 2, near)
    a = me // (2 * near)

    def index(a_, b_, c_):
        return (a_ * near + b_) * 2 + c_

    local = []
    tests_in = pltpu.make_async_copy(tests_hbm, tests, tests_sem)
    values_in = pltpu.make_async_copy(values_hbm, values, values_sem)
    basis_in = [
        pltpu.make_async_copy(basis_hbm.at[l], basis.at[l], basis_sem.at[l])
        for l in range(layers)
    ]
    docs_in = [
        pltpu.make_async_copy(
            docs_hbm.at[:, pl.ds(k * part, part)], docs.at[k], docs_sem.at[k]
        )
        for k in range(chunks)
    ]
    for copy in [tests_in, values_in] + basis_in + docs_in:
        copy.start()

    barrier = pltpu.get_barrier_semaphore()

    def greet(i):
        pl.semaphore_signal(
            barrier, inc=1, device_id={"blk": lax.rem(me + 1 + i, n)}, device_id_type=MESH
        )

    repeat(n - 1, greet)

    def copy_of(k, block, slot, target):
        return pltpu.make_async_remote_copy(
            src_ref=ready.at[k, block],
            dst_ref=ready.at[k, block],
            send_sem=send_sem.at[k, slot],
            recv_sem=recv_sem.at[k, block],
            device_id={"blk": target},
            device_id_type=MESH,
        )

    def arrived(k, block):
        copy_of(k, block, block, me).wait_recv()

    def to_core(k, block):
        copy_of(k, block, block + 1 - 2 * c, index(a, b, 1 - c)).start()

    def to_near(k, a_):
        def one(i):
            b_ = lax.rem(b + 1 + i, near)
            copy_of(k, index(a_, b, c), index(a_, b_, c), index(a, b_, c)).start()

        repeat(near - 1, one)

    def send_own(k):
        def one(i):
            a_ = lax.rem(a + 1 + i, far)
            copy_of(k, me, index(a_, b, c), index(a_, b, c)).start()

        repeat(far - 1, one)
        to_near(k, a)
        to_core(k, me)

    def pass_far(k):
        def one(i):
            a_ = lax.rem(a + 1 + i, far)
            arrived(k, index(a_, b, c))
            to_near(k, a_)
            to_core(k, index(a_, b, c))

        repeat(far - 1, one)

    def pass_near(k):
        def outer(j):
            a_ = lax.rem(a + j, far)

            def one(i):
                block = index(a_, lax.rem(b + 1 + i, near), c)
                arrived(k, block)
                to_core(k, block)

            repeat(near - 1, one)

        repeat(far, outer)

    def finish(k):
        repeat(far * near, lambda i: arrived(k, 2 * i + 1 - c))

    def multiply(k):
        docs_in[k].wait()
        doc = docs[k].astype(jnp.bfloat16)

        def one(i):
            rows_at = pl.ds(i * TILE, TILE)
            block = ready[k, pl.ds(i * (TILE // rows), TILE // rows)].reshape(TILE, part)
            product = lax.dot_general(block, doc, NT, preferred_element_type=jnp.float32)
            if k == 0:
                acc[rows_at, :] = product
            else:
                acc[rows_at, :] += product

        repeat(queries // TILE, one)

    tests_in.wait()
    values_in.wait()
    pieces = chunks // layers
    for l in range(layers):
        level = values[l : l + 1, :]
        damping = 0.1 * jnp.mean(level)
        mine = split3(tests[:, l * width : (l + 1) * width])
        basis_in[l].wait()
        turned = jnp.dot(mine, basis[l], preferred_element_type=jnp.float32)
        turned = turned[:rows] + (turned[rows : 2 * rows] + turned[2 * rows :])
        turned = split3(turned / (level + damping))
        for p in range(pieces):
            k = l * pieces + p
            back = lax.dot_general(
                turned, basis[l, p * part : (p + 1) * part, :], NT,
                preferred_element_type=jnp.float32,
            )
            back = back[:rows] + (back[rows : 2 * rows] + back[2 * rows :])
            ready[k, me] = back.astype(jnp.bfloat16)
            if k == 0:
                pl.semaphore_wait(barrier, n - 1)
            send_own(k)

    for step in range(chunks + 2):
        if step < chunks:
            pass_far(step)
        if 1 <= step <= chunks:
            pass_near(step - 1)
        if step >= 2:
            finish(step - 2)
            multiply(step - 2)

    lanes = 128

    def square(i):
        rows_at = pl.ds(i * TILE, TILE)
        raw = acc[rows_at, :]
        raw = raw * raw
        folded = raw[:, :lanes]
        for j in range(1, raw.shape[1] // lanes):
            folded = folded + raw[:, j * lanes : (j + 1) * lanes]
        sums[me, i] = jnp.sum(folded.T, axis=0, keepdims=True)

    repeat(queries // TILE, square)

    def sums_copy(block, slot, target):
        return pltpu.make_async_remote_copy(
            src_ref=sums.at[block],
            dst_ref=sums.at[block],
            send_sem=sums_send.at[slot],
            recv_sem=sums_recv.at[block],
            device_id={"blk": target},
            device_id_type=MESH,
        )

    def tell(i):
        other = lax.rem(me + 1 + i, n)
        sums_copy(me, other, other).start()

    repeat(n - 1, tell)

    def sent(i):
        other = lax.rem(me + 1 + i, n)
        for k in range(chunks):
            copy_of(k, other, other, other).wait_send()

    repeat(n - 1, sent)

    def heard(i):
        other = lax.rem(me + 1 + i, n)
        sums_copy(other, other, other).wait_recv()

    repeat(n - 1, heard)

    def scale(i):
        rows_at = pl.ds(i * TILE, TILE)
        spread = jnp.sum(sums[:, i], axis=0) / total_docs
        factor = 1.0 / jnp.sqrt(spread + 1e-06)
        factor = jnp.broadcast_to(factor, (lanes, TILE)).T
        for j in range(acc.shape[1] // lanes):
            acc[rows_at, j * lanes : (j + 1) * lanes] *= factor
        pltpu.make_async_copy(acc.at[rows_at], out_hbm.at[rows_at], out_sem.at[i]).start()

    repeat(queries // TILE, scale)

    def written(i):
        rows_at = pl.ds(i * TILE, TILE)
        pltpu.make_async_copy(acc.at[rows_at], out_hbm.at[rows_at], out_sem.at[i]).wait()

    repeat(queries // TILE, written)

    def told(i):
        other = lax.rem(me + 1 + i, n)
        sums_copy(me, other, other).wait_send()

    repeat(n - 1, told)


def shards(n, doc_grads, test_grads, eigen_basis, eigen_values):
    docs, columns = doc_grads.shape
    rows = test_grads.shape[0]
    layers, width = eigen_values.shape
    chips = n // 2
    near = 1
    while near * near * 4 <= chips:
        near *= 2
    far = chips // near
    chunks = layers * PIECES
    part = columns // chunks
    queries = n * rows
    anywhere = pl.BlockSpec(memory_space=pl.ANY)
    dma = pltpu.SemaphoreType.DMA
    return pl.pallas_call(
        functools.partial(kernel, far, near),
        out_shape=jax.ShapeDtypeStruct((queries, docs), jnp.float32),
        in_specs=[anywhere] * 4,
        out_specs=anywhere,
        scratch_shapes=[
            pltpu.VMEM((chunks, docs, part), jnp.float32),
            pltpu.VMEM((rows, columns), jnp.float32),
            pltpu.VMEM((layers, width, width), jnp.bfloat16),
            pltpu.VMEM((layers, width), jnp.float32),
            pltpu.VMEM((chunks, n, rows, part), jnp.bfloat16),
            pltpu.VMEM((queries, docs), jnp.float32),
            pltpu.VMEM((n, queries // TILE, 1, TILE), jnp.float32),
            dma((chunks,)),
            dma,
            dma((layers,)),
            dma,
            dma((queries // TILE,)),
            dma((chunks, n)),
            dma((chunks, n)),
            dma((n,)),
            dma((n,)),
        ],
        compiler_params=pltpu.CompilerParams(
            collective_id=0, has_side_effects=True, vmem_limit_bytes=50 * 2**20
        ),
        cost_estimate=pl.CostEstimate(
            flops=2 * queries * docs * columns, bytes_accessed=4 * docs * columns, transcendentals=0
        ),
    )(doc_grads, test_grads, eigen_basis, eigen_values)


def solution(mesh):
    in_specs = (P(("grp", "blk"), None), P(("grp", "blk"), None), P(), P())
    out_specs = P(None, ("grp", "blk"))
    return jax.shard_map(
        functools.partial(shards, mesh.shape["blk"]),
        mesh=mesh, in_specs=in_specs, out_specs=out_specs, check_vma=False,
    )
```

time: 106 us -> 29.1 us (0.27)
  waiting for transfers between devices: 43.6 us -> 0 us
  blocking collectives: 31.4 us -> 0 us
  Pallas kernels: 0 us -> 26.4 us
  between operations: 14.7 us -> 0.01 us
  matrix products: 12.8 us -> 0 us
  other arithmetic: 3.23 us -> 0 us
  local copies, waits for them, and re-layouts: 0.02 us -> 2.48 us
    all_gather x1 -> x0, waiting for transfers between devices: 42.9 us -> none  [shards(): lax.all_gather(test_grads, 'blk', axis=0, tiled=True)]
    psum x1 -> x0, blocking collectives: 31.4 us -> none  [shards(): squares = lax.psum(local_squares, 'blk')]
    pallas_call x0 -> x1, Pallas kernels: none -> 26.4 us  [shards(): pl.pallas_call(functools.partial(kernel, far, near), out_shape=jax.ShapeD...]
    dot_general x5 -> x0, matrix products: 12.8 us -> none  [the longest x2 5.69 us: precondition(): jnp.dot(part, basis, precision=lax.Precision.HIGHEST, preferred_element_t...]
    unnamed x8 -> x5, local copies, waits for them, and re-layouts: 0.02 us -> 2.48 us
    reduce_sum x1 -> x0, other arithmetic: 1.42 us -> none  [precondition(): damping = 0.1 * jnp.mean(values)]
  transfers between devices with their start and end apart: 1 -> 0, of which waited for: 1 -> 0; matrix products, arithmetic and copies ran while one was open for 2% -> 0% of each run, Pallas kernels for 0% -> 0%
where the time goes in v1:
time: 29.1 us; the launch traced here: 28.9 us
  Pallas kernels  26.4 us (91%)
  local copies, waits for them, and re-layouts  2.48 us (9%)
    pallas_call x1, Pallas kernels, shards(): pl.pallas_call(functools.partial(kernel, far, near), out_shape=jax.ShapeD...  26.4 us
    unnamed x5, local copies, waits for them, and re-layouts  2.48 us

profile of v1, /device:TPU:0, one launch (start us, length us, event | category | flops | bytes accessed | tf_op | source)
XLA Modules:
  0.0 28.9 jit_solution(15610763928509371686)
XLA Ops:
  0.0 0.0 copy-start
  0.0 0.9 %copy-done = f32[16,2048]{1,0:T(8,128)S(1)} copy-done((f32[16,2048]{1,0:T(8,128)S(1)}, f32[16,2048]{1,0:T(8,128)}, u32[]{:S(2)}) %copy-start) | copy-done | bytes 131096
  0.9 0.0 copy-start.1
  0.9 0.7 %copy-done.1 = f32[2,1024]{1,0:T(2,128)S(1)} copy-done((f32[2,1024]{1,0:T(2,128)S(1)}, f32[2,1024]{1,0:T(2,128)}, u32[]{:S(2)}) %copy-start.1) | copy-done | bytes 8216
  1.6 26.4 %shard_map.46 = f32[256,768]{1,0:T(8,128)S(1)} custom-call(f32[768,2048]{1,0:T(8,128)} %docs_hbm.1, f32[16,2048]{1,0:T(8,128)S(1)} %copy-done, bf16[2,1024,1024]{2,1,0:T(8,128)(2,1)} %basis_hbm.1, f32[2,1024]{1,0:T(2,128)S(1)} %copy-done.1), custom_call_target="tpu_custom_call" | custom-call | flops 805306368 | bytes 6291456 | tf_op jit(solution)/shard_map/pallas_call | solution.py:260
  28.0 0.9 %copy.6 = f32[256,768]{1,0:T(8,128)} copy(f32[256,768]{1,0:T(8,128)S(1)} %shard_map.46) | data formatting | bytes 1572864
Async XLA Ops:
  0.0 0.9 %copy-start = (f32[16,2048]{1,0:T(8,128)S(1)}, f32[16,2048]{1,0:T(8,128)}, u32[]{:S(2)}) copy-start(f32[16,2048]{1,0:T(8,128)} %tests_hbm.1) | copy-start | bytes 393220
  0.9 0.7 %copy-start.1 = (f32[2,1024]{1,0:T(2,128)S(1)}, f32[2,1024]{1,0:T(2,128)}, u32[]{:S(2)}) copy-start(f32[2,1024]{1,0:T(2,128)} %values_hbm.1) | copy-start | bytes 24580

commit v2 on v1

v2 whole, which is shorter than its diff:
```python
import functools

import jax
import jax.numpy as jnp
from jax import lax
from jax.experimental import pallas as pl
from jax.experimental.pallas import tpu as pltpu
from jax.sharding import PartitionSpec as P

PIECES = 1
DIRECT = 0
TILE = 256
LANES = 128
MESH = pl.DeviceIdType.MESH
NT = (((1,), (1,)), ((), ()))


def repeat(count, body):
    if count <= 16:
        for i in range(count):
            body(i)
    else:
        lax.fori_loop(0, count, lambda i, c: (body(i), c)[1], 0)


def split3(x):
    high = x.astype(jnp.bfloat16)
    rest = x - high.astype(jnp.float32)
    mid = rest.astype(jnp.bfloat16)
    low = (rest - mid.astype(jnp.float32)).astype(jnp.bfloat16)
    return jnp.concatenate([high, mid, low], axis=0)


def kernel(
    docs_hbm, tests_hbm, basis_hbm, values_hbm, raw,
    docs, tests, basis, values, ready, sums,
    docs_sem, tests_sem, basis_sem, values_sem,
    far_send, far_recv, near_send, near_recv, core_send, core_recv,
    sums_send, sums_recv,
):
    layers, width = values.shape
    chunks, _, near, far, rows, part = ready.shape
    n = far * near * 2
    total_docs = n * docs.shape[1]
    queries = n * rows
    tiles = queries // TILE
    me = lax.axis_index("blk")
    c = lax.rem(me, 2)
    b = lax.rem(me // 2, near)
    a = me // (2 * near)

    def index(a_, b_, c_):
        return (a_ * near + b_) * 2 + c_

    def hop(i):
        return far - 1 - i

    def other_far(i):
        return lax.rem(a + hop(i), far)

    def other_near(i):
        return lax.rem(b + 1 + i, near)

    def other(i):
        return lax.rem(me + 1 + i, n)

    tests_in = pltpu.make_async_copy(tests_hbm, tests, tests_sem)
    values_in = pltpu.make_async_copy(values_hbm, values, values_sem)
    basis_in = [
        pltpu.make_async_copy(basis_hbm.at[l], basis.at[l], basis_sem.at[l])
        for l in range(layers)
    ]
    docs_in = [
        pltpu.make_async_copy(
            docs_hbm.at[:, pl.ds(k * part, part)], docs.at[k], docs_sem.at[k]
        )
        for k in range(chunks)
    ]
    for copy in [tests_in, values_in] + basis_in:
        copy.start()

    barrier = pltpu.get_barrier_semaphore()

    def greet(target):
        pl.semaphore_signal(barrier, inc=1, device_id={"blk": target}, device_id_type=MESH)

    repeat(n - 1, lambda i: greet(other(i)))

    def far_copy(k, a_, source):
        return pltpu.make_async_remote_copy(
            src_ref=ready.at[k, c, b, source],
            dst_ref=ready.at[k, c, b, source],
            send_sem=far_send.at[k, a_],
            recv_sem=far_recv.at[k, source],
            device_id={"blk": index(a_, b, c)},
            device_id_type=MESH,
        )

    def near_copy(k, b_, a_, source):
        return pltpu.make_async_remote_copy(
            src_ref=ready.at[k, c, source, a_],
            dst_ref=ready.at[k, c, source, a_],
            send_sem=near_send.at[k, b_, a_],
            recv_sem=near_recv.at[k, source, a_],
            device_id={"blk": index(a, b_, c)},
            device_id_type=MESH,
        )

    def core_copy(k, b_, source):
        return pltpu.make_async_remote_copy(
            src_ref=ready.at[k, source, b_],
            dst_ref=ready.at[k, source, b_],
            send_sem=core_send.at[k, b_],
            recv_sem=core_recv.at[k, b_],
            device_id={"blk": index(a, b, 1 - c)},
            device_id_type=MESH,
        )

    def to_near(k, a_):
        repeat(near - 1, lambda i: near_copy(k, other_near(i), a_, b).start())

    def direct_copy(k, a_, b_):
        return pltpu.make_async_remote_copy(
            src_ref=ready.at[k, c, b, a],
            dst_ref=ready.at[k, c, b, a],
            send_sem=near_send.at[k, b_, a_],
            recv_sem=near_recv.at[k, b, a],
            device_id={"blk": index(a_, b_, c)},
            device_id_type=MESH,
        )

    def send_own(k):
        repeat(far - 1, lambda i: far_copy(k, other_far(i), a).start())
        if k < chunks - DIRECT:
            to_near(k, a)
        else:
            repeat(
                far,
                lambda j: repeat(
                    near - 1,
                    lambda i: direct_copy(k, lax.rem(a + 1 + j, far), other_near(i)).start(),
                ),
            )

    def pass_far(k):
        def one(i):
            a_ = lax.rem(a + far - hop(i), far)
            far_copy(k, a, a_).wait_recv()
            if k < chunks - DIRECT:
                to_near(k, a_)

        repeat(far - 1, one)
        core_copy(k, b, c).start()

    def pass_near(k):
        def one(i):
            b_ = other_near(i)
            repeat(far, lambda j: near_copy(k, b, lax.rem(a + j, far), b_).wait_recv())
            core_copy(k, b_, c).start()

        repeat(near - 1, one)

    def multiply(k):
        repeat(near, lambda i: core_copy(k, i, 1 - c).wait_recv())
        docs_in[k].wait()
        doc = docs[k].astype(jnp.bfloat16)
        blocks = TILE // rows

        def one(i):
            rows_at = pl.ds(i * TILE, TILE)
            parts = []
            for j in range(blocks):
                place = i * blocks + j
                parts.append(ready[k, place % 2, place // 2 % near, place // (2 * near)])
            block = jnp.concatenate(parts, axis=0)
            product = lax.dot_general(block, doc, NT, preferred_element_type=jnp.float32)
            if k > 0:
                product = raw[rows_at, :] + product
            raw[rows_at, :] = product
            if k == chunks - 1:
                square = product * product
                folded = square[:, :LANES]
                for j in range(1, square.shape[1] // LANES):
                    folded = folded + square[:, j * LANES : (j + 1) * LANES]
                sums[me, i] = jnp.sum(folded.T, axis=0, keepdims=True)

        repeat(tiles, one)

    tests_in.wait()
    values_in.wait()
    pieces = chunks // layers
    for l in range(layers):
        level = values[l : l + 1, :]
        damping = 0.1 * jnp.mean(level)
        mine = split3(tests[:, l * width : (l + 1) * width])
        basis_in[l].wait()
        if l == layers - 1:
            for copy in docs_in:
                copy.start()
        turned = jnp.dot(mine, basis[l], preferred_element_type=jnp.float32)
        turned = turned[:rows] + (turned[rows : 2 * rows] + turned[2 * rows :])
        turned = split3(turned / (level + damping))
        for p in range(pieces):
            k = l * pieces + p
            back = lax.dot_general(
                turned, basis[l, p * part : (p + 1) * part, :], NT,
                preferred_element_type=jnp.float32,
            )
            back = back[:rows] + (back[rows : 2 * rows] + back[2 * rows :])
            ready[k, c, b, a] = back.astype(jnp.bfloat16)
            if k == 0:
                pl.semaphore_wait(barrier, n - 1)
            send_own(k)

    for k in range(chunks):
        pass_far(k)
    for k in range(chunks):
        pass_near(k)
        if k > 0:
            multiply(k - 1)
    multiply(chunks - 1)

    def sums_copy(source, target):
        return pltpu.make_async_remote_copy(
            src_ref=sums.at[source],
            dst_ref=sums.at[source],
            send_sem=sums_send.at[target],
            recv_sem=sums_recv.at[source],
            device_id={"blk": target},
            device_id_type=MESH,
        )

    repeat(n - 1, lambda i: sums_copy(me, other(i)).start())

    for k in range(chunks):
        repeat(far - 1, lambda i: far_copy(k, other_far(i), a).wait_send())
        repeat(
            near - 1,
            lambda i: repeat(far, lambda j: near_copy(k, other_near(i), j, b).wait_send()),
        )
        repeat(near, lambda i: core_copy(k, i, c).wait_send())

    repeat(n - 1, lambda i: sums_copy(other(i), other(i)).wait_recv())

    def scale(i):
        rows_at = pl.ds(i * TILE, TILE)
        spread = jnp.sum(sums[:, i], axis=0) / total_docs
        factor = 1.0 / jnp.sqrt(spread + 1e-06)
        factor = jnp.broadcast_to(factor, (LANES, TILE)).T
        for j in range(raw.shape[1] // LANES):
            raw[rows_at, j * LANES : (j + 1) * LANES] *= factor

    repeat(tiles, scale)
    repeat(n - 1, lambda i: sums_copy(me, other(i)).wait_send())


def shards(n, doc_grads, test_grads, eigen_basis, eigen_values):
    docs, columns = doc_grads.shape
    rows = test_grads.shape[0]
    layers, width = eigen_values.shape
    chips = n // 2
    near = 1
    while near * near * 4 <= chips:
        near *= 2
    far = chips // near
    chunks = layers * PIECES
    part = columns // chunks
    queries = n * rows
    tiles = queries // TILE
    hbm = pl.BlockSpec(memory_space=pltpu.HBM)
    dma = pltpu.SemaphoreType.DMA
    return pl.pallas_call(
        kernel,
        out_shape=jax.ShapeDtypeStruct((queries, docs), jnp.float32),
        in_specs=[hbm] * 4,
        out_specs=pl.BlockSpec(memory_space=pltpu.VMEM),
        scratch_shapes=[
            pltpu.VMEM((chunks, docs, part), jnp.float32),
            pltpu.VMEM((rows, columns), jnp.float32),
            pltpu.VMEM((layers, width, width), jnp.bfloat16),
            pltpu.VMEM((layers, width), jnp.float32),
            pltpu.VMEM((chunks, 2, near, far, rows, part), jnp.bfloat16),
            pltpu.VMEM((n, tiles, 1, TILE), jnp.float32),
            dma((chunks,)),
            dma,
            dma((layers,)),
            dma,
            dma((chunks, far)),
            dma((chunks, far)),
            dma((chunks, near, far)),
            dma((chunks, near, far)),
            dma((chunks, near)),
            dma((chunks, near)),
            dma((n,)),
            dma((n,)),
        ],
        compiler_params=pltpu.CompilerParams(
            collective_id=0, has_side_effects=True, vmem_limit_bytes=50 * 2**20
        ),
        cost_estimate=pl.CostEstimate(
            flops=2 * queries * docs * columns, bytes_accessed=4 * docs * columns, transcendentals=0
        ),
    )(*(pltpu.with_memory_space_constraint(x, pltpu.HBM) for x in (doc_grads, test_grads, eigen_basis, eigen_values)))


def solution(mesh):
    in_specs = (P(("grp", "blk"), None), P(("grp", "blk"), None), P(), P())
    out_specs = P(None, ("grp", "blk"))
    return jax.shard_map(
        functools.partial(shards, mesh.shape["blk"]),
        mesh=mesh, in_specs=in_specs, out_specs=out_specs, check_vma=False,
    )
```

time: 29.1 us -> 24 us (0.82)
  Pallas kernels: 26.4 us -> 23 us
  local copies, waits for them, and re-layouts: 2.48 us -> 0.88 us
    pallas_call x1, Pallas kernels: 26.4 us -> 23 us  [shards(): pl.pallas_call(kernel, out_shape=jax.ShapeDtypeStruct((queries, docs), jn...]
    unnamed x5 -> x1, local copies, waits for them, and re-layouts: 2.48 us -> 0.88 us
where the time goes in v2:
time: 24 us; the launch traced here: 23.8 us
  Pallas kernels  23 us (96%)
  local copies, waits for them, and re-layouts  0.88 us (4%)
    pallas_call x1, Pallas kernels, shards(): pl.pallas_call(kernel, out_shape=jax.ShapeDtypeStruct((queries, docs), jn...  23 us
    unnamed x1, local copies, waits for them, and re-layouts  0.88 us

profile of v2, /device:TPU:0, one launch (start us, length us, event | category | flops | bytes accessed | tf_op | source)
XLA Modules:
  0.0 23.8 jit_solution(15248607531160670211)
XLA Ops:
  0.0 23.0 %shard_map.46 = f32[256,768]{1,0:T(8,128)S(1)} custom-call(f32[768,2048]{1,0:T(8,128)} %docs_hbm.1, f32[16,2048]{1,0:T(8,128)} %tests_hbm.1, bf16[2,1024,1024]{2,1,0:T(8,128)(2,1)} %basis_hbm.1, f32[2,1024]{1,0:T(2,128)} %values_hbm.1), custom_call_target="tpu_custom_call" | custom-call | flops 805306368 | bytes 6291456 | tf_op jit(solution)/shard_map/pallas_call | solution.py:272
  23.0 0.9 %copy.6 = f32[256,768]{1,0:T(8,128)} copy(f32[256,768]{1,0:T(8,128)S(1)} %shard_map.46) | data formatting | bytes 1572864

commit v3 on v2

--- a/solution.py
+++ b/solution.py
@@ -33,7 +33,7 @@
 
 def kernel(
     docs_hbm, tests_hbm, basis_hbm, values_hbm, raw,
-    docs, tests, basis, values, ready, sums,
+    docs, docs16, tests, basis, values, ready, sums,
     docs_sem, tests_sem, basis_sem, values_sem,
     far_send, far_recv, near_send, near_recv, core_send, core_recv,
     sums_send, sums_recv,
@@ -130,10 +130,12 @@
         )
 
     def send_own(k):
+        if k < chunks - DIRECT:
+            to_near(k, a)
         repeat(far - 1, lambda i: far_copy(k, other_far(i), a).start())
         if k < chunks - DIRECT:
-            to_near(k, a)
-        else:
+            return
+        if DIRECT:
             repeat(
                 far,
                 lambda j: repeat(
@@ -162,8 +164,7 @@
 
     def multiply(k):
         repeat(near, lambda i: core_copy(k, i, 1 - c).wait_recv())
-        docs_in[k].wait()
-        doc = docs[k].astype(jnp.bfloat16)
+        doc = docs16[k]
         blocks = TILE // rows
 
         def one(i):
@@ -213,6 +214,10 @@
             send_own(k)
 
     for k in range(chunks):
+        docs_in[k].wait()
+        docs16[k] = docs[k].astype(jnp.bfloat16)
+
+    for k in range(chunks):
         pass_far(k)
     for k in range(chunks):
         pass_near(k)
@@ -276,6 +281,7 @@
         out_specs=pl.BlockSpec(memory_space=pltpu.VMEM),
         scratch_shapes=[
             pltpu.VMEM((chunks, docs, part), jnp.float32),
+            pltpu.VMEM((chunks, docs, part), jnp.bfloat16),
             pltpu.VMEM((rows, columns), jnp.float32),
             pltpu.VMEM((layers, width, width), jnp.bfloat16),
             pltpu.VMEM((layers, width), jnp.float32),

time: 24 us -> 24 us (level)
  no operation moved by 1% of the time
where the time goes in v3:
time: 24 us; the launch traced here: 23.9 us
  Pallas kernels  23 us (96%)
  local copies, waits for them, and re-layouts  0.88 us (4%)
    pallas_call x1, Pallas kernels, shards(): pl.pallas_call(kernel, out_shape=jax.ShapeDtypeStruct((queries, docs), jn...  23 us
    unnamed x1, local copies, waits for them, and re-layouts  0.88 us

profile of v3, /device:TPU:0, one launch (start us, length us, event | category | flops | bytes accessed | tf_op | source)
XLA Modules:
  0.0 23.9 jit_solution(14460815223518004011)
XLA Ops:
  0.0 23.0 %shard_map.46 = f32[256,768]{1,0:T(8,128)S(1)} custom-call(f32[768,2048]{1,0:T(8,128)} %docs_hbm.1, f32[16,2048]{1,0:T(8,128)} %tests_hbm.1, bf16[2,1024,1024]{2,1,0:T(8,128)(2,1)} %basis_hbm.1, f32[2,1024]{1,0:T(2,128)} %values_hbm.1), custom_call_target="tpu_custom_call" | custom-call | flops 805306368 | bytes 6291456 | tf_op jit(solution)/shard_map/pallas_call | solution.py:277
  23.0 0.9 %copy.6 = f32[256,768]{1,0:T(8,128)} copy(f32[256,768]{1,0:T(8,128)S(1)} %shard_map.46) | data formatting | bytes 1572864
